TPU v7x, 256 devices: a whole 4x4x8 slice. The times are simulated.
256 devices in a mesh: rows: 64 (over x_hi, y, z), cols: 4 (over x_lo, core).
Axes of the slice: x: 4 (x_hi: 2, x_lo: 2; x = x_hi * 2 + x_lo), y: 4, z: 8, core: 2. Of those that a mesh axis runs over, the one named last changes fastest.
Arguments:
- features: float32 [32768, 512], P('rows', 'cols'), may hold values from -6 to 6
- weight_one: float32 [512, 512], P(None, 'cols'), may hold values from -0.25 to 0.25
- weight_two: float32 [512, 512], P(None, 'cols'), may hold values from -0.25 to 0.25
- head_col: float32 [2, 64, 512, 512], P(None, 'rows'), may hold values from -0.125 to 0.125
- diag: float32 [2, 64, 512, 512], P(None, 'rows'), may hold values from -0.125 to 0.125
- head_row: float32 [2, 64, 512, 512], P(None, 'rows'), may hold values from -0.0234375 to 0.0234375
- occupancy: int32 [2, 64, 3], P(None, 'rows'), may hold values 0 or 1
- counts: int32 [2, 64], replicated, may hold values from 1 to 512, 24576 in all within a row
- vertex_lists: int32 [2, 32768], P(None, 'rows'), may hold values from 0 to 32767, as said below
Outputs:
- hidden_two: float32 [32768, 512], P('rows', 'cols')
Inputs may be any that keep to these rules, and one draw needn't show every extreme that they name: For each term, vertex_lists[t] is a permutation of 0 to 32767, and the 512 slots of every block row name exactly 8 vertices of every block row.
All inputs are finite; a program needn't handle non-finite values. No bound on the sum of `occupancy` on one device may be relied on, other than what follows from the above.
Results may differ from a plain program's by a relative error of at most 0.0001.
Values sent between devices are 32-bit elements; how exact they have to be, the bound alone decides.
A program may use at most 64 MiB of HBM per device.

v0:
```python
import jax
import jax.numpy as jnp
from jax import lax
from jax.experimental import pallas as pl
from jax.experimental.pallas import tpu as pltpu
from jax.sharding import PartitionSpec as P

MESH = pl.DeviceIdType.MESH
F32 = jnp.float32
BF16 = jnp.bfloat16
ROWS = 64
COLS = 4
TILE = 512
WIDTH = 128
GROUP = 8
BOTH = 2 * GROUP
CHUNKS = 4
PART = TILE // CHUNKS


def dot(a, b):
    return lax.dot_general(a, b, (((1,), (0,)), ((), ())), preferred_element_type=F32)


def dot_nt(a, b):
    return lax.dot_general(a, b, (((1,), (1,)), ((), ())), preferred_element_type=F32)


def iota(shape, dim):
    return lax.broadcasted_iota(jnp.int32, shape, dim)


def onehot(cond):
    return jnp.where(cond, 1.0, 0.0).astype(BF16)


def halves(value):
    high = value.astype(BF16)
    low = (value - high.astype(F32)).astype(BF16)
    return high, low


def side(value):
    return jnp.concatenate(halves(value), axis=1)


def total(product):
    return product[:, :WIDTH] + product[:, WIDTH:]


def kernel(
    x_ref, w1_ref, w2_ref, hc_ref, dg_ref, hr_ref, occ_ref, cnt_ref, vl_ref,
    o_ref,
    tiles, fold, place, pick, pick_t, idx_out, idx_in, first_out, first_in, w1_all, w1_cat,
    send, arrived, head, back_out, back, part, part_y, sum_y, part_z, sum_z, part_x, wide,
    tile_sem, idx_s, idx_r, first_s, first_r, w_s, w_r, a_s, a_r, h_s, h_r, b_s, b_r, p_s, p_r,
    c_s, c_r,
):
    me = lax.axis_index("rows")
    col = lax.axis_index("cols")
    mx, my, mz = me // 32, (me // 8) % 4, me % 8
    spot = (my * 8 + mz) * 2 + mx

    def remote(src, dst, s, r, row, column):
        return pltpu.make_async_remote_copy(
            src, dst, s, r, device_id=(row, column), device_id_type=MESH
        )

    def peer(j):
        return lax.rem(me + j, ROWS)

    def col_peer(bit):
        core, low = col % 2, col // 2
        if bit & 1:
            core = 1 - core
        if bit & 2:
            low = 1 - low
        return low * 2 + core

    barrier = pltpu.get_barrier_semaphore()

    @pl.loop(1, ROWS)
    def _(j):
        pl.semaphore_signal(barrier, inc=1, device_id=(peer(j), col), device_id_type=MESH)

    for bit in (1, 2, 3):
        pl.semaphore_signal(barrier, inc=1, device_id=(me, col_peer(bit)), device_id_type=MESH)

    loads = []
    for k, ref in enumerate((dg_ref, hc_ref, hr_ref)):
        copy = pltpu.make_async_copy(ref, tiles.at[k], tile_sem.at[k])
        copy.start()
        loads.append(copy)

    upper = onehot(iota((TILE, TILE), 0) < iota((TILE, TILE), 1))
    request = jnp.zeros((ROWS, 128), F32)
    for t in range(2):
        lists = vl_ref[t : t + 1, :]
        source = lists >> 9
        local = lists & 511
        owner = iota((ROWS, TILE), 0) == source
        mask = onehot(owner)
        before = dot(mask, upper)
        rank = jnp.sum(jnp.where(owner, before, 0.0), axis=0, keepdims=True).astype(jnp.int32)
        lane = iota((128, TILE), 0) == rank + t * GROUP
        high = jnp.where(lane, (local >> 1).astype(F32), 0.0).astype(BF16)
        low = jnp.where(lane, (local & 1).astype(F32), 0.0).astype(BF16)
        request = request + 2.0 * dot_nt(mask, high) + dot_nt(mask, low)
        live = iota((1, TILE), 1) < cnt_ref[t, me]
        grouped = source * GROUP + rank
        place[t] = onehot((iota((TILE, TILE), 0) == grouped) & live)
        first_out[t : t + 1, :] = (((source & 31) * 2 + (source >> 5)) * GROUP + rank).astype(F32)
    for b in range(ROWS):
        idx_out[b] = request[b : b + 1, :]

    pl.semaphore_wait(barrier, ROWS - 1 + COLS - 1)

    @pl.loop(1, ROWS)
    def _(j):
        p = peer(j)
        remote(idx_out.at[p], idx_in.at[me], idx_s, idx_r, p, col).start()

    @pl.when(me == 0)
    def _():
        @pl.loop(1, ROWS)
        def _(j):
            remote(first_out, first_in, first_s, first_r, j, col).start()

        first_in[...] = first_out[...]

    idx_in[me] = idx_out[me]
    w1_all[col] = w1_ref[...]
    for bit in (1, 2, 3):
        remote(
            w1_ref, w1_all.at[col], w_s.at[bit - 1], w_r.at[bit - 1], me, col_peer(bit)
        ).start()

    def folded(k, t, rows, cols):
        flag = occ_ref[t, 0, k].astype(F32)
        i = 2 * k + t
        spread = dot(place[rows], side_wide(tiles[k, t] * flag)).astype(BF16)
        both = jnp.concatenate([spread[:, :TILE], spread[:, TILE:]], axis=0)
        fold[i] = dot_nt(both, place[cols]).astype(BF16)

    def side_wide(value):
        return jnp.concatenate(halves(value), axis=1)

    flag_of = {0: 0, 1: 1, 2: 2}
    loads[0].wait()
    for t in range(2):
        folded(flag_of[0], t, t, t)

    pltpu.make_async_copy(
        idx_in.at[pl.ds(0, ROWS - 1)], idx_in.at[pl.ds(0, ROWS - 1)], idx_r
    ).wait()
    asked = jnp.concatenate([idx_in[b] for b in range(ROWS)], axis=0)
    asked_high = (asked.astype(jnp.int32) >> 1).astype(F32)
    asked_low = asked - 2.0 * asked_high
    asked_high, asked_low = asked_high.astype(BF16), asked_low.astype(BF16)
    count = ROWS * BOTH
    repeat = onehot((iota((count, ROWS), 0) >> 4) == iota((count, ROWS), 1))
    keep = (iota((count, 128), 0) & 15) == iota((count, 128), 1)
    ones = jnp.ones((128, TILE), F32).astype(BF16)
    column = 2.0 * dot(
        jnp.where(keep, dot(repeat, asked_high), 0.0).astype(BF16), ones
    ) + dot(jnp.where(keep, dot(repeat, asked_low), 0.0).astype(BF16), ones)
    pick[...] = onehot(column.astype(jnp.int32) == iota((count, TILE), 1))

    def run(layer, rows):
        send[layer] = total(dot(pick[...], side(rows))).reshape(ROWS, BOTH, WIDTH)
        head[layer, spot] = send[layer, 0]
        other = (1 - mx) * 32 + my * 8 + mz
        hx = remote(
            send.at[layer, 0], head.at[layer, spot], h_s.at[layer, 0], h_r.at[layer, 0], other, col
        )
        hx.start()

        @pl.loop(1, ROWS)
        def _(j):
            p = peer(j)
            remote(
                send.at[layer, p], arrived.at[layer, me], a_s.at[layer], a_r.at[layer], p, col
            ).start()

        arrived[layer, me] = send[layer, me]

        if layer == 0:
            lane_of = onehot(iota((128, count), 0) == (iota((128, count), 1) & 15))
            block_of = iota((ROWS, count), 0) == (iota((ROWS, count), 1) >> 4)
            spread = 2.0 * dot(asked_high, lane_of) + dot(asked_low, lane_of)
            line = jnp.sum(jnp.where(block_of, spread, 0.0), axis=0, keepdims=True)
            pick_t[...] = onehot(iota((TILE, count), 0) == line.astype(jnp.int32))

        hx.wait_recv()
        pair = (my * 8 + mz) * 2
        for d in range(1, 8):
            z = (mz + d) % 8
            remote(
                head.at[layer, pl.ds(pair, 2)], head.at[layer, pl.ds(pair, 2)],
                h_s.at[layer, 1], h_r.at[layer, 1], mx * 32 + my * 8 + z, col,
            ).start()

        if layer == 0:
            @pl.when(me != 0)
            def _():
                pltpu.make_async_copy(first_in, first_in, first_r).wait()

            for t in range(2):
                live = iota((1, TILE), 1) < cnt_ref[t, 0]
                line = first_in[t : t + 1, :].astype(jnp.int32)
                place[2 + t] = onehot((iota((TILE, TILE), 0) == line) & live)
            loads[2].wait()
            for t in range(2):
                folded(2, t, 2 + t, t)

        area = head.at[layer, pl.ds(0, 14)]
        pltpu.make_async_copy(area, area, h_r.at[layer, 1]).wait()
        for d in range(1, 4):
            y = (my + d) % 4
            remote(
                head.at[layer, pl.ds(my * 16, 16)], head.at[layer, pl.ds(my * 16, 16)],
                h_s.at[layer, 2], h_r.at[layer, 2], mx * 32 + y * 8 + mz, col,
            ).start()

        if layer == 0:
            loads[1].wait()
            for t in range(2):
                folded(1, t, t, 2 + t)

        area = arrived.at[layer, pl.ds(0, ROWS - 1)]
        pltpu.make_async_copy(area, area, a_r.at[layer]).wait()

        def product(i, right):
            both = dot(fold[i], right)
            return total(both[:TILE] + both[TILE:])

        rights = []
        for t in range(2):
            got = arrived[layer, :, t * GROUP : (t + 1) * GROUP, :].reshape(TILE, WIDTH)
            rights.append(side(got))
            across = product(4 + t, rights[t])
            part[layer, :, t * GROUP : (t + 1) * GROUP, :] = across.reshape(ROWS, GROUP, WIDTH)
        for d in range(1, 4):
            y = (my + d) % 4
            remote(
                part.at[layer, pl.ds(y * 16, 16)], part_y.at[layer, d - 1],
                p_s.at[layer, 0], p_r.at[layer, 0], mx * 32 + y * 8 + mz, col,
            ).start()
        blocks = [product(t, rights[t]) for t in range(2)]

        area = head.at[layer, pl.ds(0, 48)]
        pltpu.make_async_copy(area, area, h_r.at[layer, 2]).wait()
        for t in range(2):
            first = head[layer, :, t * GROUP : (t + 1) * GROUP, :].reshape(TILE, WIDTH)
            block = blocks[t] + product(2 + t, side(first))
            back_out[layer, :, t * GROUP : (t + 1) * GROUP, :] = block.reshape(ROWS, GROUP, WIDTH)

        @pl.loop(1, ROWS)
        def _(j):
            p = peer(j)
            remote(
                back_out.at[layer, p], back.at[layer, me], b_s.at[layer], b_r.at[layer], p, col
            ).start()

        back[layer, me] = back_out[layer, me]

        pltpu.make_async_copy(part_y.at[layer], part_y.at[layer], p_r.at[layer, 0]).wait()
        sum_y[layer] = (
            part[layer, pl.ds(my * 16, 16)]
            + part_y[layer, 0] + part_y[layer, 1] + part_y[layer, 2]
        )
        for d in range(1, 8):
            z = (mz + d) % 8
            remote(
                sum_y.at[layer, pl.ds(z * 2, 2)], part_z.at[layer, d - 1],
                p_s.at[layer, 1], p_r.at[layer, 1], mx * 32 + my * 8 + z, col,
            ).start()
        pltpu.make_async_copy(part_z.at[layer], part_z.at[layer], p_r.at[layer, 1]).wait()
        gathered = sum_y[layer, pl.ds(mz * 2, 2)]
        for d in range(7):
            gathered = gathered + part_z[layer, d]
        sum_z[layer] = gathered
        px = remote(
            sum_z.at[layer, 1 - mx], part_x.at[layer], p_s.at[layer, 2], p_r.at[layer, 2],
            other, col,
        )
        px.start()
        px.wait_recv()
        extra = sum_z[layer, mx] + part_x[layer]

        area = back.at[layer, pl.ds(0, ROWS - 1)]
        pltpu.make_async_copy(area, area, b_r.at[layer]).wait()
        back[layer, 0] = back[layer, 0] + extra
        return total(dot(pick_t[...], side(back[layer].reshape(count, WIDTH))))

    mine = run(0, x_ref[...])

    wide[col] = mine
    near, far, across = col_peer(1), col_peer(2), col_peer(3)
    for k in range(CHUNKS):
        rows = pl.ds(k * PART, PART)
        remote(
            wide.at[col, rows], wide.at[col, rows], c_s.at[0, k], c_r.at[0, k], me, far
        ).start()
    remote(wide.at[col], wide.at[col], c_s.at[1, 0], c_r.at[1, 0], me, near).start()
    for bit in (1, 2, 3):
        remote(
            w1_ref, w1_all.at[col], w_s.at[bit - 1], w_r.at[bit - 1], me, col_peer(bit)
        ).wait()
    for c in range(COLS):
        high, low = halves(w1_all[c])
        w1_cat[:, c * WIDTH : (c + 1) * WIDTH] = high
        w1_cat[:, TILE + c * WIDTH : TILE + (c + 1) * WIDTH] = low
    for k in range(CHUNKS):
        rows = pl.ds(k * PART, PART)
        remote(
            wide.at[col, rows], wide.at[far, rows], c_s.at[0, k], c_r.at[0, k], me, far
        ).wait_recv()
        remote(
            wide.at[far, rows], wide.at[far, rows], c_s.at[2, k], c_r.at[2, k], me, near
        ).start()
    remote(wide.at[col], wide.at[near], c_s.at[1, 0], c_r.at[1, 0], me, near).wait_recv()
    for k in range(CHUNKS):
        rows = pl.ds(k * PART, PART)
        remote(
            wide.at[far, rows], wide.at[across, rows], c_s.at[2, k], c_r.at[2, k], me, near
        ).wait_recv()
    high, low = halves(jnp.concatenate([wide[c] for c in range(COLS)], axis=1))
    both = dot(high, w1_cat[...])
    hidden = both[:, :TILE] + both[:, TILE:] + dot(low, w1_cat[:, :TILE])
    high, low = halves(jnp.maximum(hidden, 0.0))
    w2 = side(w2_ref[...])
    z = total(dot(high, w2)) + dot(low, w2[:, :WIDTH])

    o_ref[...] = jnp.maximum(run(1, z), 0.0)

    def drain(ref, sem):
        pltpu.make_async_copy(ref, ref, sem).wait()

    drain(idx_in.at[pl.ds(0, ROWS - 1)], idx_s)

    @pl.when(me == 0)
    def _():
        @pl.loop(1, ROWS)
        def _(j):
            drain(first_out, first_s)

    for layer in range(2):
        drain(arrived.at[layer, pl.ds(0, ROWS - 1)], a_s.at[layer])
        drain(back.at[layer, pl.ds(0, ROWS - 1)], b_s.at[layer])
        drain(head.at[layer, 0], h_s.at[layer, 0])
        drain(head.at[layer, pl.ds(0, 14)], h_s.at[layer, 1])
        drain(head.at[layer, pl.ds(0, 48)], h_s.at[layer, 2])
        drain(part_y.at[layer], p_s.at[layer, 0])
        drain(part_z.at[layer], p_s.at[layer, 1])
        drain(part_x.at[layer], p_s.at[layer, 2])
    drain(wide.at[0], c_s.at[1, 0])
    for k in range(CHUNKS):
        drain(wide.at[0, pl.ds(0, PART)], c_s.at[0, k])
        drain(wide.at[0, pl.ds(0, PART)], c_s.at[2, k])


def shards(
    features, weight_one, weight_two, head_col, diag, head_row, occupancy, counts, vertex_lists
):
    terms = vertex_lists.shape[0]
    vmem = pl.BlockSpec(memory_space=pltpu.VMEM)
    smem = pl.BlockSpec(memory_space=pltpu.SMEM)
    hbm = pl.BlockSpec(memory_space=pl.ANY)
    count = ROWS * BOTH
    dma = pltpu.SemaphoreType.DMA

    def rows(*lead):
        return pltpu.VMEM(lead + (BOTH, WIDTH), F32)

    return pl.pallas_call(
        kernel,
        out_shape=jax.ShapeDtypeStruct((TILE, WIDTH), F32),
        in_specs=[vmem, vmem, vmem, hbm, hbm, hbm, smem, smem, vmem],
        out_specs=vmem,
        scratch_shapes=[
            pltpu.VMEM((3, terms, TILE, TILE), F32),
            pltpu.VMEM((3 * terms, 2 * TILE, TILE), BF16),
            pltpu.VMEM((2 * terms, TILE, TILE), BF16),
            pltpu.VMEM((count, TILE), BF16),
            pltpu.VMEM((TILE, count), BF16),
            pltpu.VMEM((ROWS, 1, 128), F32),
            pltpu.VMEM((ROWS, 1, 128), F32),
            pltpu.VMEM((terms, TILE), F32),
            pltpu.VMEM((terms, TILE), F32),
            pltpu.VMEM((COLS, TILE, WIDTH), F32),
            pltpu.VMEM((TILE, 2 * TILE), BF16),
            rows(2, ROWS), rows(2, ROWS), rows(2, ROWS), rows(2, ROWS), rows(2, ROWS),
            rows(2, ROWS), rows(2, 3, 16), rows(2, 16), rows(2, 7, 2), rows(2, 2), rows(2),
            pltpu.VMEM((COLS, TILE, WIDTH), F32),
            dma((3,)), dma, dma, dma, dma, dma((3,)), dma((3,)),
            dma((2,)), dma((2,)), dma((2, 3)), dma((2, 3)), dma((2,)), dma((2,)),
            dma((2, 3)), dma((2, 3)), dma((3, CHUNKS)), dma((3, CHUNKS)),
        ],
        compiler_params=pltpu.CompilerParams(
            collective_id=0, has_side_effects=True, vmem_limit_bytes=56 << 20
        ),
    )(
        features, weight_one, weight_two,
        head_col.reshape(terms, TILE, TILE), diag.reshape(terms, TILE, TILE),
        head_row.reshape(terms, TILE, TILE), occupancy, counts, vertex_lists,
    )


def solution(mesh):
    in_specs = (
        P("rows", "cols"),
        P(None, "cols"),
        P(None, "cols"),
        P(None, "rows", None, None),
        P(None, "rows", None, None),
        P(None, "rows", None, None),
        P(None, "rows", None),
        P(),
        P(None, "rows"),
    )
    out_specs = P("rows", "cols")
    return jax.shard_map(shards, mesh=mesh, in_specs=in_specs, out_specs=out_specs, check_vma=False)
```

profile of v0, /device:TPU:6, one launch (start us, length us, event | category | flops | bytes accessed | tf_op | source)
XLA Modules:
  0.0 126.8 jit_solution(17028070602997342411)
XLA Ops:
  0.0 125.2 %shard_map.91 = f32[512,128]{1,0:T(8,128)} custom-call(f32[512,128]{1,0:T(8,128)} %x_ref.1, f32[512,128]{1,0:T(8,128)} %w1_ref.1, f32[512,128]{1,0:T(8,128)} %w2_ref.1, f32[2,512,512]{2,1,0:T(8,128)} %bitcast.3, f32[2,512,512]{2,1,0:T(8,128)} %bitcast.4, f32[2,512,512]{2,1,0:T(8,128)} %bitcast.5, s32[2,1,3]{2,1,0:T(1,128)} %occ_ref.1, s32[2,64]{1,0:T(2,128)} %cnt_ref.1, ...), custom_call_target="tpu_custom_call" | custom-call | tf_op jit(solution)/shard_map/pallas_call | solution.py:376
  125.2 1.7 %copy.11 = f32[512,128]{1,0:T(8,128)} copy(f32[512,128]{1,0:T(8,128)} %shard_map.91) | data formatting | bytes 524288
where the time goes:
time: 127 us
  Pallas kernels  125 us (98%)
  local copies, waits for them, and re-layouts  1.67 us (1%)
    pallas_call x1, Pallas kernels, shards(): pl.pallas_call(kernel, out_shape=jax.ShapeDtypeStruct((TILE, WIDTH), F32)...  125 us

commit v1 on v0

v1 whole, which is shorter than its diff:
```python
import jax
import jax.numpy as jnp
from jax import lax
from jax.experimental import pallas as pl
from jax.experimental.pallas import tpu as pltpu
from jax.sharding import PartitionSpec as P

MESH = pl.DeviceIdType.MESH
F32 = jnp.float32
BF16 = jnp.bfloat16
ROWS = 64
COLS = 4
TILE = 512
WIDTH = 128
GROUP = 8
BOTH = 2 * GROUP
CHUNKS = 4
PART = TILE // CHUNKS
HALF = TILE // 2


def dot(a, b):
    return lax.dot_general(a, b, (((1,), (0,)), ((), ())), preferred_element_type=F32)


def dot_nt(a, b):
    return lax.dot_general(a, b, (((1,), (1,)), ((), ())), preferred_element_type=F32)


def iota(shape, dim):
    return lax.broadcasted_iota(jnp.int32, shape, dim)


def onehot(cond):
    return jnp.where(cond, 1.0, 0.0).astype(BF16)


def halves(value):
    high = value.astype(BF16)
    low = (value - high.astype(F32)).astype(BF16)
    return high, low


def side(value):
    return jnp.concatenate(halves(value), axis=1)


def total(product):
    return product[:, :WIDTH] + product[:, WIDTH:]


def kernel(
    x_ref, w1_ref, w2_ref, hc_ref, dg_ref, hr_ref, occ_ref, cnt_ref, vl_ref,
    o_ref,
    tiles, fold, place, pick, pick_t, idx_out, idx_in, first_out, first_in, w1_all, w1_cat,
    send, arrived, first_rows, head, back_out, back, part, part_y, sum_y, part_z, wide,
    tile_sem, idx_s, idx_r, first_s, first_r, w_s, w_r, a_s, a_r, h_s, h_r, b_s, b_r, p_s, p_r,
    c_s, c_r,
):
    me = lax.axis_index("rows")
    col = lax.axis_index("cols")
    mx, my, mz = me // 32, (me // 8) % 4, me % 8
    line_of = me - mz

    def remote(src, dst, s, r, row, column):
        return pltpu.make_async_remote_copy(
            src, dst, s, r, device_id=(row, column), device_id_type=MESH
        )

    def fold_out(i, size):
        return size // 2 + jnp.where(i % 2 == 0, i // 2, -((i + 1) // 2))

    def peer(j):
        x = (mx + 1 - j // 32) % 2
        y = (my + fold_out((j // 8) % 4, 4)) % 4
        z = (mz + fold_out(j % 8, 8)) % 8
        return x * 32 + y * 8 + z

    def along(j):
        return line_of + (mz + fold_out(j, 8)) % 8

    def plane(j):
        return ((mx + 1 - j // 4) % 2) * 32 + ((my + fold_out(j % 4, 4)) % 4) * 8 + mz

    def col_peer(bit):
        core, low = col % 2, col // 2
        if bit & 1:
            core = 1 - core
        if bit & 2:
            low = 1 - low
        return low * 2 + core

    barrier = pltpu.get_barrier_semaphore()

    @pl.loop(0, ROWS - 1)
    def _(j):
        pl.semaphore_signal(barrier, inc=1, device_id=(peer(j), col), device_id_type=MESH)

    for bit in (1, 2, 3):
        pl.semaphore_signal(barrier, inc=1, device_id=(me, col_peer(bit)), device_id_type=MESH)

    loads = []
    for k, ref in enumerate((dg_ref, hc_ref, hr_ref)):
        copy = pltpu.make_async_copy(ref, tiles.at[k], tile_sem.at[k])
        copy.start()
        loads.append(copy)

    upper = onehot(iota((TILE, TILE), 0) < iota((TILE, TILE), 1))
    request = jnp.zeros((ROWS, 128), F32)
    for t in range(2):
        lists = vl_ref[t : t + 1, :]
        source = lists >> 9
        local = lists & 511
        owner = iota((ROWS, TILE), 0) == source
        mask = onehot(owner)
        before = dot(mask, upper)
        rank = jnp.sum(jnp.where(owner, before, 0.0), axis=0, keepdims=True).astype(jnp.int32)
        lane = iota((128, TILE), 0) == rank + t * GROUP
        high = jnp.where(lane, (local >> 1).astype(F32), 0.0).astype(BF16)
        low = jnp.where(lane, (local & 1).astype(F32), 0.0).astype(BF16)
        request = request + 2.0 * dot_nt(mask, high) + dot_nt(mask, low)
        live = iota((1, TILE), 1) < cnt_ref[t, me]
        grouped = source * GROUP + rank
        place[t] = onehot((iota((TILE, TILE), 0) == grouped) & live)
        first_out[t : t + 1, :] = grouped.astype(F32)
    for b in range(ROWS):
        idx_out[b] = request[b : b + 1, :]

    def folded(k, t, rows, cols):
        flag = occ_ref[t, 0, k].astype(F32)
        i = 2 * k + t
        spread = dot(place[rows], side(tiles[k, t] * flag)).astype(BF16)
        both = jnp.concatenate([spread[:, :TILE], spread[:, TILE:]], axis=0)
        fold[i] = dot_nt(both, place[cols]).astype(BF16)

    loads[0].wait()
    for t in range(2):
        folded(0, t, t, t)

    pl.semaphore_wait(barrier, ROWS - 1 + COLS - 1)

    @pl.loop(0, ROWS - 1)
    def _(j):
        p = peer(j)
        remote(idx_out.at[p], idx_in.at[me], idx_s, idx_r, p, col).start()

    @pl.when(me == 0)
    def _():
        @pl.loop(1, ROWS)
        def _(j):
            remote(first_out, first_in, first_s, first_r, j, col).start()

        first_in[...] = first_out[...]

    idx_in[me] = idx_out[me]
    near, far, across = col_peer(1), col_peer(2), col_peer(3)
    w1_all[col] = w1_ref[...]
    remote(w1_ref, w1_all.at[col], w_s.at[1], w_r.at[1], me, far).start()
    remote(w1_ref, w1_all.at[col], w_s.at[0], w_r.at[0], me, near).start()

    pltpu.make_async_copy(
        idx_in.at[pl.ds(0, ROWS - 1)], idx_in.at[pl.ds(0, ROWS - 1)], idx_r
    ).wait()
    asked = jnp.concatenate([idx_in[b] for b in range(ROWS)], axis=0)
    asked_high = (asked.astype(jnp.int32) >> 1).astype(F32)
    asked_low = asked - 2.0 * asked_high
    asked_high, asked_low = asked_high.astype(BF16), asked_low.astype(BF16)
    count = ROWS * BOTH
    repeat = onehot((iota((count, ROWS), 0) >> 4) == iota((count, ROWS), 1))
    keep = (iota((count, 128), 0) & 15) == iota((count, 128), 1)
    ones = jnp.ones((128, TILE), F32).astype(BF16)
    column = 2.0 * dot(
        jnp.where(keep, dot(repeat, asked_high), 0.0).astype(BF16), ones
    ) + dot(jnp.where(keep, dot(repeat, asked_low), 0.0).astype(BF16), ones)
    pick[...] = onehot(column.astype(jnp.int32) == iota((count, TILE), 1))

    def run(layer, rows):
        right = side(rows)
        own = total(dot(pick[0:BOTH, :], right))
        first_rows[layer] = own
        head[layer, me] = own

        @pl.loop(0, 7)
        def _(j):
            remote(
                first_rows.at[layer], head.at[layer, me], h_s.at[layer, 0], h_r.at[layer, 0],
                along(j), col,
            ).start()

        for part_of in range(2):
            half = (mx + 1 - part_of) % 2
            area = pl.ds(pl.multiple_of(half * TILE, TILE), TILE)
            blocks = pl.ds(half * 32, 32)
            send[layer, blocks] = total(dot(pick[area, :], right)).reshape(32, BOTH, WIDTH)

            @pl.loop(part_of * 32, part_of * 31 + 32)
            def _(j):
                p = peer(j)
                remote(
                    send.at[layer, p], arrived.at[layer, me], a_s.at[layer], a_r.at[layer], p, col
                ).start()

        arrived[layer, me] = send[layer, me]

        if layer == 0:
            remote(w1_ref, w1_all.at[far], w_s.at[1], w_r.at[1], me, far).wait_recv()
            remote(w1_all.at[far], w1_all.at[far], w_s.at[2], w_r.at[2], me, near).start()
            lane_of = onehot(iota((128, count), 0) == (iota((128, count), 1) & 15))
            block_of = iota((ROWS, count), 0) == (iota((ROWS, count), 1) >> 4)
            spread = 2.0 * dot(asked_high, lane_of) + dot(asked_low, lane_of)
            line = jnp.sum(jnp.where(block_of, spread, 0.0), axis=0, keepdims=True)
            pick_t[...] = onehot(iota((TILE, count), 0) == line.astype(jnp.int32))

        area = head.at[layer, pl.ds(0, 7)]
        pltpu.make_async_copy(area, area, h_r.at[layer, 0]).wait()

        @pl.loop(0, 7)
        def _(j):
            line = head.at[layer, pl.ds(line_of, 8)]
            remote(line, line, h_s.at[layer, 1], h_r.at[layer, 1], plane(j), col).start()

        if layer == 0:
            @pl.when(me != 0)
            def _():
                pltpu.make_async_copy(first_in, first_in, first_r).wait()

            for t in range(2):
                live = iota((1, TILE), 1) < cnt_ref[t, 0]
                line = first_in[t : t + 1, :].astype(jnp.int32)
                place[2 + t] = onehot((iota((TILE, TILE), 0) == line) & live)
            loads[2].wait()
            for t in range(2):
                folded(2, t, 2 + t, t)
            loads[1].wait()
            for t in range(2):
                folded(1, t, t, 2 + t)

        area = arrived.at[layer, pl.ds(0, ROWS - 1)]
        pltpu.make_async_copy(area, area, a_r.at[layer]).wait()

        def product(i, right):
            both = dot(fold[i], right)
            return total(both[:TILE] + both[TILE:])

        rights = []
        for t in range(2):
            got = arrived[layer, :, t * GROUP : (t + 1) * GROUP, :].reshape(TILE, WIDTH)
            rights.append(side(got))
            across = product(4 + t, rights[t])
            part[layer, :, t * GROUP : (t + 1) * GROUP, :] = across.reshape(ROWS, GROUP, WIDTH)

        @pl.loop(0, 7)
        def _(j):
            p = plane(j)
            remote(
                part.at[layer, pl.ds(p - mz, 8)], part_y.at[layer, j],
                p_s.at[layer, 0], p_r.at[layer, 0], p, col,
            ).start()

        blocks = [product(t, rights[t]) for t in range(2)]

        area = head.at[layer, pl.ds(0, 56)]
        pltpu.make_async_copy(area, area, h_r.at[layer, 1]).wait()
        for t in range(2):
            first = head[layer, :, t * GROUP : (t + 1) * GROUP, :].reshape(TILE, WIDTH)
            block = blocks[t] + product(2 + t, side(first))
            back_out[layer, :, t * GROUP : (t + 1) * GROUP, :] = block.reshape(ROWS, GROUP, WIDTH)

        @pl.loop(0, ROWS - 1)
        def _(j):
            p = peer(j)
            remote(
                back_out.at[layer, p], back.at[layer, me], b_s.at[layer], b_r.at[layer], p, col
            ).start()

        back[layer, me] = back_out[layer, me]

        pltpu.make_async_copy(part_y.at[layer], part_y.at[layer], p_r.at[layer, 0]).wait()
        gathered = part[layer, pl.ds(line_of, 8)]
        for d in range(7):
            gathered = gathered + part_y[layer, d]
        sum_y[layer] = gathered

        @pl.loop(0, 7)
        def _(j):
            p = along(j)
            remote(
                sum_y.at[layer, p % 8], part_z.at[layer, j],
                p_s.at[layer, 1], p_r.at[layer, 1], p, col,
            ).start()

        area = back.at[layer, pl.ds(0, ROWS - 1)]
        pltpu.make_async_copy(area, area, b_r.at[layer]).wait()
        right = side(back[layer].reshape(count, WIDTH))
        sums = [dot(pick_t[k * HALF : (k + 1) * HALF, :], right) for k in range(2)]

        pltpu.make_async_copy(part_z.at[layer], part_z.at[layer], p_r.at[layer, 1]).wait()
        extra = sum_y[layer, mz]
        for d in range(7):
            extra = extra + part_z[layer, d]
        filled = jnp.concatenate([extra, jnp.zeros((WIDTH - BOTH, WIDTH), F32)], axis=0)
        right = side(filled)
        return [
            total(sums[k] + dot(pick_t[k * HALF : (k + 1) * HALF, :WIDTH], right))
            for k in range(2)
        ]

    mine = run(0, x_ref[...])

    def chunk(k):
        return pl.ds(k * PART, PART)

    for k in range(CHUNKS):
        if k % 2 == 0:
            wide[col, pl.ds(k * PART, HALF)] = mine[k // 2]
        remote(
            wide.at[col, chunk(k)], wide.at[col, chunk(k)], c_s.at[0, k], c_r.at[0, k], me, far
        ).start()
    for k in range(CHUNKS):
        remote(
            wide.at[col, chunk(k)], wide.at[col, chunk(k)], c_s.at[1, k], c_r.at[1, k], me, near
        ).start()
    remote(w1_ref, w1_all.at[near], w_s.at[0], w_r.at[0], me, near).wait_recv()
    remote(w1_ref, w1_all.at[across], w_s.at[2], w_r.at[2], me, near).wait_recv()
    for c in range(COLS):
        high, low = halves(w1_all[c])
        w1_cat[:, c * WIDTH : (c + 1) * WIDTH] = high
        w1_cat[:, TILE + c * WIDTH : TILE + (c + 1) * WIDTH] = low
    w2 = side(w2_ref[...])
    mixed = []
    for h in range(2):
        for k in (2 * h, 2 * h + 1):
            remote(
                wide.at[col, chunk(k)], wide.at[far, chunk(k)], c_s.at[0, k], c_r.at[0, k], me, far
            ).wait_recv()
            remote(
                wide.at[far, chunk(k)], wide.at[far, chunk(k)], c_s.at[2, k], c_r.at[2, k], me, near
            ).start()
        for k in (2 * h, 2 * h + 1):
            for step, c in ((1, near), (2, across)):
                remote(
                    wide.at[c, chunk(k)], wide.at[c, chunk(k)], c_s.at[step, k], c_r.at[step, k],
                    me, near,
                ).wait_recv()
        rows = slice(h * HALF, (h + 1) * HALF)
        high, low = halves(jnp.concatenate([wide[c, rows] for c in range(COLS)], axis=1))
        both = dot(high, w1_cat[...])
        hidden = both[:, :TILE] + both[:, TILE:] + dot(low, w1_cat[:, :TILE])
        high, low = halves(jnp.maximum(hidden, 0.0))
        mixed.append(total(dot(high, w2)) + dot(low, w2[:, :WIDTH]))

    for k, value in enumerate(run(1, jnp.concatenate(mixed, axis=0))):
        o_ref[k * HALF : (k + 1) * HALF, :] = jnp.maximum(value, 0.0)

    def drain(ref, sem):
        pltpu.make_async_copy(ref, ref, sem).wait()

    drain(idx_in.at[pl.ds(0, ROWS - 1)], idx_s)

    @pl.when(me == 0)
    def _():
        @pl.loop(1, ROWS)
        def _(j):
            drain(first_out, first_s)

    for layer in range(2):
        drain(arrived.at[layer, pl.ds(0, ROWS - 1)], a_s.at[layer])
        drain(back.at[layer, pl.ds(0, ROWS - 1)], b_s.at[layer])
        drain(head.at[layer, pl.ds(0, 7)], h_s.at[layer, 0])
        drain(head.at[layer, pl.ds(0, 56)], h_s.at[layer, 1])
        drain(part_y.at[layer], p_s.at[layer, 0])
        drain(part_z.at[layer], p_s.at[layer, 1])
    for k in range(3):
        drain(w1_ref, w_s.at[k])
    for k in range(CHUNKS):
        for step in range(3):
            drain(wide.at[0, pl.ds(0, PART)], c_s.at[step, k])


def shards(
    features, weight_one, weight_two, head_col, diag, head_row, occupancy, counts, vertex_lists
):
    terms = vertex_lists.shape[0]
    vmem = pl.BlockSpec(memory_space=pltpu.VMEM)
    smem = pl.BlockSpec(memory_space=pltpu.SMEM)
    hbm = pl.BlockSpec(memory_space=pl.ANY)
    count = ROWS * BOTH
    dma = pltpu.SemaphoreType.DMA

    def rows(*lead):
        return pltpu.VMEM(lead + (BOTH, WIDTH), F32)

    return pl.pallas_call(
        kernel,
        out_shape=jax.ShapeDtypeStruct((TILE, WIDTH), F32),
        in_specs=[vmem, vmem, vmem, hbm, hbm, hbm, smem, smem, vmem],
        out_specs=vmem,
        scratch_shapes=[
            pltpu.VMEM((3, terms, TILE, TILE), F32),
            pltpu.VMEM((3 * terms, 2 * TILE, TILE), BF16),
            pltpu.VMEM((2 * terms, TILE, TILE), BF16),
            pltpu.VMEM((count, TILE), BF16),
            pltpu.VMEM((TILE, count), BF16),
            pltpu.VMEM((ROWS, 1, 128), F32),
            pltpu.VMEM((ROWS, 1, 128), F32),
            pltpu.VMEM((terms, TILE), F32),
            pltpu.VMEM((terms, TILE), F32),
            pltpu.VMEM((COLS, TILE, WIDTH), F32),
            pltpu.VMEM((TILE, 2 * TILE), BF16),
            rows(2, ROWS), rows(2, ROWS), rows(2), rows(2, ROWS), rows(2, ROWS), rows(2, ROWS),
            rows(2, ROWS), rows(2, 7, 8), rows(2, 8), rows(2, 7),
            pltpu.VMEM((COLS, TILE, WIDTH), F32),
            dma((3,)), dma, dma, dma, dma, dma((3,)), dma((3,)),
            dma((2,)), dma((2,)), dma((2, 2)), dma((2, 2)), dma((2,)), dma((2,)),
            dma((2, 2)), dma((2, 2)), dma((3, CHUNKS)), dma((3, CHUNKS)),
        ],
        compiler_params=pltpu.CompilerParams(
            collective_id=0, has_side_effects=True, vmem_limit_bytes=56 << 20
        ),
    )(
        features, weight_one, weight_two,
        head_col.reshape(terms, TILE, TILE), diag.reshape(terms, TILE, TILE),
        head_row.reshape(terms, TILE, TILE), occupancy, counts, vertex_lists,
    )


def solution(mesh):
    in_specs = (
        P("rows", "cols"),
        P(None, "cols"),
        P(None, "cols"),
        P(None, "rows", None, None),
        P(None, "rows", None, None),
        P(None, "rows", None, None),
        P(None, "rows", None),
        P(),
        P(None, "rows"),
    )
    out_specs = P("rows", "cols")
    return jax.shard_map(shards, mesh=mesh, in_specs=in_specs, out_specs=out_specs, check_vma=False)
```

time: 127 us -> 101 us (0.80)
  Pallas kernels: 125 us -> 99.3 us
    pallas_call x1, Pallas kernels: 125 us -> 99.3 us  [shards(): pl.pallas_call(kernel, out_shape=jax.ShapeDtypeStruct((TILE, WIDTH), F32)...]
where the time goes in v1:
time: 101 us
  Pallas kernels  99.3 us (98%)
  local copies, waits for them, and re-layouts  1.67 us (2%)
    pallas_call x1, Pallas kernels, shards(): pl.pallas_call(kernel, out_shape=jax.ShapeDtypeStruct((TILE, WIDTH), F32)...  99.3 us

profile of v1, /device:TPU:6, one launch (start us, length us, event | category | flops | bytes accessed | tf_op | source)
XLA Modules:
  0.0 101.0 jit_solution(10709428291646625583)
XLA Ops:
  0.0 99.3 %shard_map.91 = f32[512,128]{1,0:T(8,128)} custom-call(f32[512,128]{1,0:T(8,128)} %x_ref.1, f32[512,128]{1,0:T(8,128)} %w1_ref.1, f32[512,128]{1,0:T(8,128)} %w2_ref.1, f32[2,512,512]{2,1,0:T(8,128)} %bitcast.3, f32[2,512,512]{2,1,0:T(8,128)} %bitcast.4, f32[2,512,512]{2,1,0:T(8,128)} %bitcast.5, s32[2,1,3]{2,1,0:T(1,128)} %occ_ref.1, s32[2,64]{1,0:T(2,128)} %cnt_ref.1, ...), custom_call_target="tpu_custom_call" | custom-call | tf_op jit(solution)/shard_map/pallas_call | solution.py:393
  99.3 1.7 %copy.11 = f32[512,128]{1,0:T(8,128)} copy(f32[512,128]{1,0:T(8,128)} %shard_map.91) | data formatting | bytes 524288

commit v2 on v1

--- a/solution.py
+++ b/solution.py
@@ -92,7 +92,7 @@
 
     barrier = pltpu.get_barrier_semaphore()
 
-    @pl.loop(0, ROWS - 1)
+    @pl.loop(0, ROWS - 1, unroll=True)
     def _(j):
         pl.semaphore_signal(barrier, inc=1, device_id=(peer(j), col), device_id_type=MESH)
 
@@ -139,7 +139,7 @@
 
     pl.semaphore_wait(barrier, ROWS - 1 + COLS - 1)
 
-    @pl.loop(0, ROWS - 1)
+    @pl.loop(0, ROWS - 1, unroll=True)
     def _(j):
         p = peer(j)
         remote(idx_out.at[p], idx_in.at[me], idx_s, idx_r, p, col).start()
@@ -180,7 +180,7 @@
         first_rows[layer] = own
         head[layer, me] = own
 
-        @pl.loop(0, 7)
+        @pl.loop(0, 7, unroll=True)
         def _(j):
             remote(
                 first_rows.at[layer], head.at[layer, me], h_s.at[layer, 0], h_r.at[layer, 0],
@@ -193,7 +193,7 @@
             blocks = pl.ds(half * 32, 32)
             send[layer, blocks] = total(dot(pick[area, :], right)).reshape(32, BOTH, WIDTH)
 
-            @pl.loop(part_of * 32, part_of * 31 + 32)
+            @pl.loop(part_of * 32, part_of * 31 + 32, unroll=True)
             def _(j):
                 p = peer(j)
                 remote(
@@ -214,7 +214,7 @@
         area = head.at[layer, pl.ds(0, 7)]
         pltpu.make_async_copy(area, area, h_r.at[layer, 0]).wait()
 
-        @pl.loop(0, 7)
+        @pl.loop(0, 7, unroll=True)
         def _(j):
             line = head.at[layer, pl.ds(line_of, 8)]
             remote(line, line, h_s.at[layer, 1], h_r.at[layer, 1], plane(j), col).start()
@@ -249,7 +249,7 @@
             across = product(4 + t, rights[t])
             part[layer, :, t * GROUP : (t + 1) * GROUP, :] = across.reshape(ROWS, GROUP, WIDTH)
 
-        @pl.loop(0, 7)
+        @pl.loop(0, 7, unroll=True)
         def _(j):
             p = plane(j)
             remote(
@@ -266,7 +266,7 @@
             block = blocks[t] + product(2 + t, side(first))
             back_out[layer, :, t * GROUP : (t + 1) * GROUP, :] = block.reshape(ROWS, GROUP, WIDTH)
 
-        @pl.loop(0, ROWS - 1)
+        @pl.loop(0, ROWS - 1, unroll=True)
         def _(j):
             p = peer(j)
             remote(
@@ -281,7 +281,7 @@
             gathered = gathered + part_y[layer, d]
         sum_y[layer] = gathered
 
-        @pl.loop(0, 7)
+        @pl.loop(0, 7, unroll=True)
         def _(j):
             p = along(j)
             remote(

time: 101 us -> 96.6 us (0.956)
  Pallas kernels: 99.3 us -> 94.7 us
    pallas_call x1, Pallas kernels: 99.3 us -> 94.7 us  [shards(): pl.pallas_call(kernel, out_shape=jax.ShapeDtypeStruct((TILE, WIDTH), F32)...]
where the time goes in v2:
time: 96.6 us; the launch traced here: 96.4 us
  Pallas kernels  94.7 us (98%)
  local copies, waits for them, and re-layouts  1.67 us (2%)
    pallas_call x1, Pallas kernels, shards(): pl.pallas_call(kernel, out_shape=jax.ShapeDtypeStruct((TILE, WIDTH), F32)...  94.7 us

profile of v2, /device:TPU:6, one launch (start us, length us, event | category | flops | bytes accessed | tf_op | source)
XLA Modules:
  0.0 96.4 jit_solution(13852142206375399169)
XLA Ops:
  0.0 94.7 %shard_map.91 = f32[512,128]{1,0:T(8,128)} custom-call(f32[512,128]{1,0:T(8,128)} %x_ref.1, f32[512,128]{1,0:T(8,128)} %w1_ref.1, f32[512,128]{1,0:T(8,128)} %w2_ref.1, f32[2,512,512]{2,1,0:T(8,128)} %bitcast.3, f32[2,512,512]{2,1,0:T(8,128)} %bitcast.4, f32[2,512,512]{2,1,0:T(8,128)} %bitcast.5, s32[2,1,3]{2,1,0:T(1,128)} %occ_ref.1, s32[2,64]{1,0:T(2,128)} %cnt_ref.1, ...), custom_call_target="tpu_custom_call" | custom-call | tf_op jit(solution)/shard_map/pallas_call | solution.py:393
  94.7 1.7 %copy.11 = f32[512,128]{1,0:T(8,128)} copy(f32[512,128]{1,0:T(8,128)} %shard_map.91) | data formatting | bytes 524288

commit v3 on v2

--- a/solution.py
+++ b/solution.py
@@ -146,7 +146,7 @@
 
     @pl.when(me == 0)
     def _():
-        @pl.loop(1, ROWS)
+        @pl.loop(1, ROWS, unroll=True)
         def _(j):
             remote(first_out, first_in, first_s, first_r, j, col).start()
 
@@ -157,6 +157,17 @@
     w1_all[col] = w1_ref[...]
     remote(w1_ref, w1_all.at[col], w_s.at[1], w_r.at[1], me, far).start()
     remote(w1_ref, w1_all.at[col], w_s.at[0], w_r.at[0], me, near).start()
+
+    def stacked(value):
+        return jnp.concatenate([value[:, :TILE], value[:, TILE:]], axis=0)
+
+    loads[1].wait()
+    loads[2].wait()
+    for t in range(2):
+        flags = [occ_ref[t, 0, k].astype(F32) for k in range(3)]
+        fold[2 + t] = stacked(dot(place[t], side(tiles[1, t] * flags[1])).astype(BF16))
+        both = jnp.concatenate(halves(tiles[2, t] * flags[2]), axis=0)
+        fold[4 + t] = dot_nt(both, place[t]).astype(BF16)
 
     pltpu.make_async_copy(
         idx_in.at[pl.ds(0, ROWS - 1)], idx_in.at[pl.ds(0, ROWS - 1)], idx_r
@@ -203,8 +214,6 @@
         arrived[layer, me] = send[layer, me]
 
         if layer == 0:
-            remote(w1_ref, w1_all.at[far], w_s.at[1], w_r.at[1], me, far).wait_recv()
-            remote(w1_all.at[far], w1_all.at[far], w_s.at[2], w_r.at[2], me, near).start()
             lane_of = onehot(iota((128, count), 0) == (iota((128, count), 1) & 15))
             block_of = iota((ROWS, count), 0) == (iota((ROWS, count), 1) >> 4)
             spread = 2.0 * dot(asked_high, lane_of) + dot(asked_low, lane_of)
@@ -220,6 +229,8 @@
             remote(line, line, h_s.at[layer, 1], h_r.at[layer, 1], plane(j), col).start()
 
         if layer == 0:
+            remote(w1_ref, w1_all.at[far], w_s.at[1], w_r.at[1], me, far).wait_recv()
+            remote(w1_all.at[far], w1_all.at[far], w_s.at[2], w_r.at[2], me, near).start()
             @pl.when(me != 0)
             def _():
                 pltpu.make_async_copy(first_in, first_in, first_r).wait()
@@ -228,12 +239,10 @@
                 live = iota((1, TILE), 1) < cnt_ref[t, 0]
                 line = first_in[t : t + 1, :].astype(jnp.int32)
                 place[2 + t] = onehot((iota((TILE, TILE), 0) == line) & live)
-            loads[2].wait()
             for t in range(2):
-                folded(2, t, 2 + t, t)
-            loads[1].wait()
-            for t in range(2):
-                folded(1, t, t, 2 + t)
+                both = jnp.concatenate([fold[4 + t, :TILE, :], fold[4 + t, TILE:, :]], axis=1)
+                fold[4 + t] = stacked(dot(place[2 + t], both).astype(BF16))
+                fold[2 + t] = dot_nt(fold[2 + t], place[2 + t]).astype(BF16)
 
         area = arrived.at[layer, pl.ds(0, ROWS - 1)]
         pltpu.make_async_copy(area, area, a_r.at[layer]).wait()
@@ -262,16 +271,18 @@
         area = head.at[layer, pl.ds(0, 56)]
         pltpu.make_async_copy(area, area, h_r.at[layer, 1]).wait()
         for t in range(2):
+            part_t = pl.ds(t * GROUP, GROUP)
             first = head[layer, :, t * GROUP : (t + 1) * GROUP, :].reshape(TILE, WIDTH)
             block = blocks[t] + product(2 + t, side(first))
             back_out[layer, :, t * GROUP : (t + 1) * GROUP, :] = block.reshape(ROWS, GROUP, WIDTH)
 
-        @pl.loop(0, ROWS - 1, unroll=True)
-        def _(j):
-            p = peer(j)
-            remote(
-                back_out.at[layer, p], back.at[layer, me], b_s.at[layer], b_r.at[layer], p, col
-            ).start()
+            @pl.loop(0, ROWS - 1, unroll=True)
+            def _(j):
+                p = peer(j)
+                remote(
+                    back_out.at[layer, p, part_t], back.at[layer, me, part_t],
+                    b_s.at[layer], b_r.at[layer], p, col,
+                ).start()
 
         back[layer, me] = back_out[layer, me]
 

time: 96.6 us -> 95.9 us (level); the launches traced: 96.4 us -> 94.7 us
  Pallas kernels: 94.7 us -> 93 us
    pallas_call x1, Pallas kernels: 94.7 us -> 93 us  [shards(): pl.pallas_call(kernel, out_shape=jax.ShapeDtypeStruct((TILE, WIDTH), F32)...]
where the time goes in v3:
time: 95.9 us; the launch traced here: 94.7 us
  Pallas kernels  93 us (97%)
  local copies, waits for them, and re-layouts  1.67 us (2%)
    pallas_call x1, Pallas kernels, shards(): pl.pallas_call(kernel, out_shape=jax.ShapeDtypeStruct((TILE, WIDTH), F32)...  93 us

profile of v3, /device:TPU:6, one launch (start us, length us, event | category | flops | bytes accessed | tf_op | source)
XLA Modules:
  0.0 94.7 jit_solution(4677989044567753956)
XLA Ops:
  0.0 93.0 %shard_map.91 = f32[512,128]{1,0:T(8,128)} custom-call(f32[512,128]{1,0:T(8,128)} %x_ref.1, f32[512,128]{1,0:T(8,128)} %w1_ref.1, f32[512,128]{1,0:T(8,128)} %w2_ref.1, f32[2,512,512]{2,1,0:T(8,128)} %bitcast.3, f32[2,512,512]{2,1,0:T(8,128)} %bitcast.4, f32[2,512,512]{2,1,0:T(8,128)} %bitcast.5, s32[2,1,3]{2,1,0:T(1,128)} %occ_ref.1, s32[2,64]{1,0:T(2,128)} %cnt_ref.1, ...), custom_call_target="tpu_custom_call" | custom-call | tf_op jit(solution)/shard_map/pallas_call | solution.py:404
  93.0 1.7 %copy.11 = f32[512,128]{1,0:T(8,128)} copy(f32[512,128]{1,0:T(8,128)} %shard_map.91) | data formatting | bytes 524288
